TPU v7x, 512 devices: a whole 4x4x16 slice. The times are simulated.
512 devices in a mesh: energy: 128 (over y, x, z_lo, core), elem: 4 (over z_hi).
Axes of the slice: x: 4, y: 4, z: 16 (z_hi: 4, z_lo: 4; z = z_hi * 4 + z_lo), core: 2. Of those that a mesh axis runs over, the one named last changes fastest.
Arguments:
- lesser_green: float32 [2, 4096, 2048], P(None, 'energy', 'elem'), may hold values from -6 to 6
- greater_green: float32 [2, 4096, 2048], P(None, 'energy', 'elem'), may hold values from -6 to 6
- partner: int32 [2048], P('elem'), may hold values from 0 to 2047, as said below
Outputs:
- lesser_polar: float32 [2, 4096, 2048], P(None, 'energy', 'elem')
- greater_polar: float32 [2, 4096, 2048], P(None, 'energy', 'elem')
Inputs may be any that keep to these rules, and one draw needn't show every extreme that they name: partner is an involution without fixed points: partner[partner[e]] = e and partner[e] != e; pairs may join elements of different groups.
All inputs are finite; a program needn't handle non-finite values.
Results may differ from a plain program's by a relative error of at most 0.000098.
Values sent between devices are 32-bit elements; how exact they have to be, the bound alone decides.
A program may use at most 64 MiB of HBM per device.

v0:
```python
import jax
import jax.numpy as jnp
import numpy as np
from jax import lax
from jax.experimental import pallas as pl
from jax.experimental.pallas import tpu as pltpu
from jax.sharding import PartitionSpec as P

PLANE, DEPTH, GROUPS, MLOC = 32, 4, 4, 32
LINE = DEPTH * GROUPS
ROWS, LANES = 256, 128
PERIOD = 8192
MESH = pl.DeviceIdType.MESH


def split(table):
    high = table.astype(jnp.bfloat16)
    low = (table - high.astype(np.float32)).astype(jnp.bfloat16)
    return high, low


def tables():
    row = np.arange(ROWS)
    plane, zl, part = row // 8, row // 2 % 4, row % 2
    index = plane // 2 * 8 + zl * 2 + plane % 2
    freq = np.arange(ROWS)
    angle = 2 * np.pi * (freq[:, None] * index[None, :] % ROWS) / ROWS
    cos, sin = np.cos(angle), np.sin(angle)
    first = np.concatenate(
        [np.where(part == 0, cos, sin), np.where(part == 0, -sin, cos)], 0
    )
    scale = 1.0 / (64 * PERIOD)
    last = scale * np.concatenate(
        [np.where(part == 0, sin, cos).T, np.where(part == 0, -cos, sin).T], 1
    )
    lane = np.arange(LANES)
    local, el = lane % MLOC, lane // MLOC
    same = (el[:, None] == el[None, :]).astype(np.float64)
    angle = 2 * np.pi * (local[:, None] * local[None, :] % MLOC) / MLOC
    cos, sin = same * np.cos(angle), same * np.sin(angle)
    middle = np.block([[cos, -sin], [sin, cos]])
    angle = 2 * np.pi * (freq[:, None] * local[None, :]) / PERIOD
    turn = np.stack([np.cos(angle), np.sin(angle)]).astype(np.float32)
    out = []
    for table in (first, middle, last):
        out.extend(split(table.astype(np.float32)))
    return [*out, turn]


def parts_of(x):
    high = x.astype(jnp.bfloat16)
    return high, (x - high.astype(jnp.float32)).astype(jnp.bfloat16)


def mm(a, b):
    return jnp.dot(a, b, preferred_element_type=jnp.float32)


def table_times(high, low, x):
    xh, xl = parts_of(x)
    return mm(high, xh) + (mm(high, xl) + mm(low, xh))


def times_table(x, high, low):
    xh, xl = parts_of(x)
    return mm(xh, high) + (mm(xl, high) + mm(xh, low))


def odd_rows(shape):
    return lax.broadcasted_iota(jnp.int32, shape, 0) % 2 == 1


def turned(real, imag, cos, sin):
    return real * cos + imag * sin, imag * cos - real * sin


def both(left, right):
    return jnp.concatenate([left, right], axis=1)


def correlate(a, b, f1h, f1l, f2h, f2l, gh, gl, turn):
    odd = odd_rows((ROWS, LANES))
    x = both(a, jnp.where(odd, -b, b))
    cos, sin = both(turn[0], turn[0]), both(turn[1], turn[1])
    y = table_times(f1h, f1l, x)
    yr, yi = turned(y[:ROWS], y[ROWS:], cos, sin)
    z = times_table(
        jnp.concatenate(
            [both(yr[:, :LANES], yi[:, :LANES]), both(yr[:, LANES:], yi[:, LANES:])], 0
        ),
        f2h,
        f2l,
    )
    ar, ai = z[:ROWS, :LANES], z[:ROWS, LANES:]
    br, bi = z[ROWS:, :LANES], z[ROWS:, LANES:]
    cr, ci = ar * br + ai * bi, ai * br - ar * bi
    v = times_table(jnp.concatenate([both(cr, ci), both(cr, -ci)], 0), f2h, f2l)
    er, ei = turned(
        both(v[:ROWS, :LANES], v[ROWS:, :LANES]),
        both(v[:ROWS, LANES:], v[ROWS:, LANES:]),
        cos,
        sin,
    )
    out = table_times(gh, gl, jnp.concatenate([er, ei], 0))
    q, p = out[:, :LANES], out[:, LANES:]
    return q, jnp.where(odd, p, -p)


def blocks_swapped(t):
    cut = [[t[32 * i : 32 * i + 32, 32 * j : 32 * j + 32] for j in range(4)] for i in range(4)]
    return [jnp.concatenate([cut[i][j] for i in range(4)], axis=1) for j in range(4)]


def to_owner(block, out):
    for part in range(2):
        t = jnp.concatenate([block(zl, part) for zl in range(4)], 0).T
        for zl, rows in enumerate(blocks_swapped(t)):
            out[:, zl * 2 + part, :] = rows


def to_energies(got, store):
    for part in range(2):
        rows = jnp.concatenate([got[:, zl * 2 + part, :] for zl in range(4)], 0)
        t = jnp.concatenate(blocks_swapped(rows), 0).T
        for zl in range(4):
            store(zl, part, t[32 * zl : 32 * zl + 32])


def permute(src, dst, order):
    def tile(d, carry):
        at = jnp.broadcast_to(order[d], (8, LANES))
        lane, where = at % LANES, at // LANES
        for part in range(2):
            total = jnp.zeros((8, LANES), jnp.float32)
            for s in range(LINE):
                piece = src[part, :, s * LANES : (s + 1) * LANES]
                moved = jnp.take_along_axis(piece, lane, axis=1)
                total = jnp.where(where == s, moved, total)
            dst[part, :, pl.ds(pl.multiple_of(d * LANES, LANES), LANES)] = total
        return carry

    lax.fori_loop(0, LINE, tile, 0)


def kernel(
    lesser, greater, partner, f1h, f1l, f2h, f2l, gh, gl, turn,
    lesser_out, greater_out,
    order, z1, swapped, z2, zl_in, send_a, send_b, own_a, own_b,
    back_q, back_p, got_q, got_p, wide_q, wide_p, z2_back, unswapped,
    sems, line_send, plane_send, few_send, local_sem,
):
    energy, zh = lax.axis_index("energy"), lax.axis_index("elem")
    w, zl = energy // 8 * 2 + energy % 2, energy // 2 % DEPTH
    z = zh * DEPTH + zl

    def device(plane, low, high):
        return {"energy": plane // 2 * 8 + low * 2 + plane % 2, "elem": high}

    def line_peer(i):
        step = i // 2 + 1
        other = (z + LINE + step * (1 - 2 * (i % 2))) % LINE
        return other % DEPTH, other // DEPTH

    def plane_peer(i):
        return (w + 1 + i) % PLANE

    barrier = pltpu.get_barrier_semaphore()

    def greet_line(i, c):
        low, high = line_peer(i)
        pl.semaphore_signal(barrier, inc=1, device_id=device(w, low, high), device_id_type=MESH)
        return c

    def greet_plane(i, c):
        pl.semaphore_signal(
            barrier, inc=1, device_id=device(plane_peer(i), zl, zh), device_id_type=MESH
        )
        return c

    lax.fori_loop(0, LINE - 1, greet_line, 0)
    lax.fori_loop(0, PLANE - 1, greet_plane, 0)
    pl.semaphore_wait(barrier, LINE - 1 + PLANE - 1)

    def remote(src, dst, send, recv, where):
        return pltpu.make_async_remote_copy(
            src_ref=src, dst_ref=dst, send_sem=send, recv_sem=recv,
            device_id=where, device_id_type=MESH,
        )

    def arrived(whole, sem):
        pltpu.make_async_copy(whole, whole, sem).wait()

    def quarter(ref, h):
        return ref.at[:, pl.ds(pl.multiple_of(h * 8, 8), 8), :]

    def lanes(ref, start, size):
        return ref.at[:, :, pl.ds(pl.multiple_of(start, LANES), size)]

    def groups(phase, src, dst, recv):
        copies = []
        for i in range(GROUPS - 1):
            h = (zh + 1 + i) % GROUPS
            copies.append(remote(src(h), dst, few_send.at[phase, i], recv, device(w, zl, h)))
        for copy in copies:
            copy.start()
        mine = pltpu.make_async_copy(src(zh), dst, recv)
        mine.start()
        return copies

    def depths(phase, src, dst, recv):
        copies = []
        for i in range(DEPTH - 1):
            low = (zl + 1 + i) % DEPTH
            copies.append(remote(src(low), dst, few_send.at[phase, i], recv, device(w, low, zh)))
        for copy in copies:
            copy.start()
        mine = pltpu.make_async_copy(src(zl), dst, recv)
        mine.start()
        return copies

    def line_copy(phase, src, dst, recv, i):
        low, high = line_peer(i)
        return remote(src(low, high), dst, line_send.at[phase, i], recv, device(w, low, high))

    def line(phase, src, dst, recv):
        def start(i, c):
            line_copy(phase, src, dst, recv, i).start()
            return c

        lax.fori_loop(0, LINE - 1, start, 0)
        pltpu.make_async_copy(src(zl, zh), dst, recv).start()

    def line_done(phase, src, dst, recv):
        def done(i, c):
            line_copy(phase, src, dst, recv, i).wait_send()
            return c

        lax.fori_loop(0, LINE - 1, done, 0)

    def plane_copy(phase, src, dst, recv, i):
        other = plane_peer(i)
        return remote(
            src.at[other], dst.at[w], plane_send.at[phase, i], recv, device(other, zl, zh)
        )

    def plane(phase, src, dst, recv):
        def start(i, c):
            plane_copy(phase, src, dst, recv, i).start()
            return c

        lax.fori_loop(0, PLANE - 1, start, 0)
        pltpu.make_async_copy(src.at[w], dst.at[w], recv).start()

    def plane_done(phase, src, dst, recv):
        def done(i, c):
            plane_copy(phase, src, dst, recv, i).wait_send()
            return c

        lax.fori_loop(0, PLANE - 1, done, 0)

    started = []
    started += groups(0, lambda h: partner, order.at[zh], sems.at[0])
    started += groups(1, lambda h: quarter(greater, h), lanes(z1, zh * 512, 512), sems.at[1])
    started += depths(2, lambda low: lanes(lesser, low * LANES, LANES), zl_in.at[zl], sems.at[2])
    arrived(zl_in, sems.at[2])
    to_owner(lambda low, part: zl_in[low, part], send_a)
    plane(0, send_a, own_a, sems.at[3])
    arrived(order, sems.at[0])
    arrived(z1, sems.at[1])
    flat = order.reshape(LINE, 1, LANES)
    permute(z1, swapped, flat)

    def swapped_src(low, high):
        return lanes(swapped, (high * DEPTH + low) * LANES, LANES)

    z2_dst = z2.at[zl, :, zh]
    line(0, swapped_src, z2_dst, sems.at[4])
    arrived(z2, sems.at[4])
    to_owner(lambda low, part: z2[low, part].reshape(MLOC, LANES), send_b)
    plane(1, send_b, own_b, sems.at[5])
    arrived(own_a, sems.at[3])
    arrived(own_b, sems.at[5])
    q, p = correlate(
        own_a[...].reshape(ROWS, LANES), own_b[...].reshape(ROWS, LANES),
        f1h[...], f1l[...], f2h[...], f2l[...], gh[...], gl[...], turn[...],
    )
    back_q[...] = q.reshape(PLANE, 8, LANES)
    plane(2, back_q, got_q, sems.at[6])
    back_p[...] = p.reshape(PLANE, 8, LANES)
    plane(3, back_p, got_p, sems.at[7])
    arrived(got_q, sems.at[6])

    def keep_q(low, part, rows):
        wide_q[low, part] = rows.reshape(GROUPS, 8, LANES)

    to_energies(got_q, keep_q)

    def wide_src(low, high):
        return wide_q.at[low, :, high]

    back_dst = lanes(z2_back, z * LANES, LANES)
    line(1, wide_src, back_dst, sems.at[8])
    arrived(got_p, sems.at[7])

    def keep_p(low, part, rows):
        wide_p[low, part] = rows

    to_energies(got_p, keep_p)
    started += depths(3, lambda low: wide_p.at[low], lanes(lesser_out, zl * LANES, LANES), sems.at[9])
    arrived(z2_back, sems.at[8])
    permute(z2_back, unswapped, flat)
    started += groups(4, lambda h: lanes(unswapped, h * 512, 512), quarter(greater_out, zh), sems.at[10])
    arrived(lesser_out, sems.at[9])
    arrived(greater_out, sems.at[10])
    for copy in started:
        copy.wait_send()
    line_done(0, swapped_src, z2_dst, sems.at[4])
    line_done(1, wide_src, back_dst, sems.at[8])
    plane_done(0, send_a, own_a, sems.at[3])
    plane_done(1, send_b, own_b, sems.at[5])
    plane_done(2, back_q, got_q, sems.at[6])
    plane_done(3, back_p, got_p, sems.at[7])


def per_device(lesser, greater, partner):
    f32 = jnp.float32
    field = jax.ShapeDtypeStruct((2, MLOC, 512), f32)
    owned = pltpu.VMEM((PLANE, 8, LANES), f32)
    long = pltpu.VMEM((2, 8, 2048), f32)
    deep = pltpu.VMEM((DEPTH, 2, MLOC, LANES), f32)
    cut = pltpu.VMEM((DEPTH, 2, GROUPS, 8, LANES), f32)
    vmem = pl.BlockSpec(memory_space=pltpu.VMEM)
    constants = [jnp.asarray(table) for table in tables()]
    return pl.pallas_call(
        kernel,
        out_shape=(field, field),
        in_specs=[vmem] * 10,
        out_specs=(vmem, vmem),
        scratch_shapes=[
            pltpu.VMEM((GROUPS, 4, 1, LANES), jnp.int32),
            long, long, cut, deep, owned, owned, owned, owned,
            owned, owned, owned, owned, cut, deep, long, long,
            pltpu.SemaphoreType.DMA((11,)),
            pltpu.SemaphoreType.DMA((2, LINE - 1)),
            pltpu.SemaphoreType.DMA((4, PLANE - 1)),
            pltpu.SemaphoreType.DMA((5, 3)),
            pltpu.SemaphoreType.DMA,
        ],
        compiler_params=pltpu.CompilerParams(
            collective_id=0, has_side_effects=True, vmem_limit_bytes=48 * 1024 * 1024
        ),
    )(lesser, greater, partner.reshape(4, 1, LANES), *constants)


def solution(mesh):
    placed = (P(None, "energy", "elem"), P(None, "energy", "elem"), P("elem"))
    return jax.shard_map(
        per_device,
        mesh=mesh,
        in_specs=placed,
        out_specs=(P(None, "energy", "elem"), P(None, "energy", "elem")),
        check_vma=False,
    )
```

profile of v0, /device:TPU:1, one launch (start us, length us, event | category | flops | bytes accessed | tf_op | source)
XLA Modules:
  0.0 92.3 jit_solution(18225640911256432018)
XLA Ops:
  0.6 0.0 copy-start
  0.6 0.9 %copy-done = f32[2,256,128]{2,1,0:T(8,128)S(1)} copy-done((f32[2,256,128]{2,1,0:T(8,128)S(1)}, f32[2,256,128]{2,1,0:T(8,128)}, u32[]{:S(2)}) %copy-start) | copy-done | bytes 262168
  1.6 0.0 copy-start.1
  1.6 0.9 %copy-done.1 = bf16[256,512]{1,0:T(8,128)(2,1)S(1)} copy-done((bf16[256,512]{1,0:T(8,128)(2,1)S(1)}, bf16[256,512]{1,0:T(8,128)(2,1)}, u32[]{:S(2)}) %copy-start.1) | copy-done | bytes 262168
  2.5 0.0 copy-start.2
  2.5 0.9 %copy-done.2 = bf16[256,512]{1,0:T(8,128)(2,1)S(1)} copy-done((bf16[256,512]{1,0:T(8,128)(2,1)S(1)}, bf16[256,512]{1,0:T(8,128)(2,1)}, u32[]{:S(2)}) %copy-start.2) | copy-done | bytes 262168
  3.5 0.0 copy-start.3
  3.5 0.9 %copy-done.3 = bf16[512,256]{1,0:T(8,128)(2,1)S(1)} copy-done((bf16[512,256]{1,0:T(8,128)(2,1)S(1)}, bf16[512,256]{1,0:T(8,128)(2,1)}, u32[]{:S(2)}) %copy-start.3) | copy-done | bytes 262168
  4.4 0.0 copy-start.4
  4.4 0.9 %copy-done.4 = bf16[512,256]{1,0:T(8,128)(2,1)S(1)} copy-done((bf16[512,256]{1,0:T(8,128)(2,1)S(1)}, bf16[512,256]{1,0:T(8,128)(2,1)}, u32[]{:S(2)}) %copy-start.4) | copy-done | bytes 262168
  5.4 0.0 copy-start.5
  5.4 0.9 copy-done.5
  6.3 0.0 copy-start.6
  6.3 0.9 copy-done.6
  7.2 0.0 copy-start.7
  7.2 0.9 copy-done.7
  8.1 0.0 copy-start.8
  8.1 0.9 copy-done.8
  9.0 0.0 copy-start.9
  9.0 0.7 copy-done.9
  9.7 81.3 %shard_map.113 = (f32[2,32,512]{2,1,0:T(8,128)S(1)}, f32[2,32,512]{2,1,0:T(8,128)S(1)}) custom-call(f32[2,32,512]{2,1,0:T(8,128)S(1)} %copy-done.5, f32[2,32,512]{2,1,0:T(8,128)S(1)} %copy-done.6, s32[4,1,128]{2,1,0:T(1,128)S(1)} %bitcast.1, bf16[512,256]{1,0:T(8,128)(2,1)S(1)} %copy-done.4, bf16[512,256]{1,0:T(8,128)(2,1)S(1)} %copy-done.3, ...), custom_call_target="tpu_custom_call" | custom-call | tf_op jit(solution)/shard_map/pallas_call | solution.py:334
  91.0 0.7 copy.14
  91.7 0.7 copy.15
Async XLA Ops:
  0.6 1.0 %copy-start = (f32[2,256,128]{2,1,0:T(8,128)S(1)}, f32[2,256,128]{2,1,0:T(8,128)}, u32[]{:S(2)}) copy-start(f32[2,256,128]{2,1,0:T(8,128)} %constant.20.clone.turn) | copy-start | bytes 786436
  1.6 0.9 %copy-start.1 = (bf16[256,512]{1,0:T(8,128)(2,1)S(1)}, bf16[256,512]{1,0:T(8,128)(2,1)}, u32[]{:S(2)}) copy-start(bf16[256,512]{1,0:T(8,128)(2,1)} %constant.19.clone.gl) | copy-start | bytes 786436
  2.5 0.9 %copy-start.2 = (bf16[256,512]{1,0:T(8,128)(2,1)S(1)}, bf16[256,512]{1,0:T(8,128)(2,1)}, u32[]{:S(2)}) copy-start(bf16[256,512]{1,0:T(8,128)(2,1)} %constant.18.clone.gh) | copy-start | bytes 786436
  3.5 0.9 %copy-start.3 = (bf16[512,256]{1,0:T(8,128)(2,1)S(1)}, bf16[512,256]{1,0:T(8,128)(2,1)}, u32[]{:S(2)}) copy-start(bf16[512,256]{1,0:T(8,128)(2,1)} %constant.15.clone.f1l) | copy-start | bytes 786436
  4.4 0.9 %copy-start.4 = (bf16[512,256]{1,0:T(8,128)(2,1)S(1)}, bf16[512,256]{1,0:T(8,128)(2,1)}, u32[]{:S(2)}) copy-start(bf16[512,256]{1,0:T(8,128)(2,1)} %constant.14.clone.f1h) | copy-start | bytes 786436
  5.4 0.9 copy-start.5
  6.3 0.9 copy-start.6
  7.2 0.9 copy-start.7
  8.1 0.9 copy-start.8
  9.0 0.7 copy-start.9
where the time goes:
time: 92.7 us; the launch traced here: 92.3 us
  Pallas kernels  81.3 us (88%)
  local copies, waits for them, and re-layouts  10.4 us (11%)
    pallas_call x1, Pallas kernels, per_device(): pl.pallas_call(kernel, out_shape=(field, field), in_specs=[vmem] * 10, ou...  81.3 us
    unnamed x22, local copies, waits for them, and re-layouts  10.4 us

commit v1 on v0

v1 whole, which is shorter than its diff:
```python
import jax
import jax.numpy as jnp
import numpy as np
from jax import lax
from jax.experimental import pallas as pl
from jax.experimental.pallas import tpu as pltpu
from jax.sharding import PartitionSpec as P

PLANE, DEPTH, GROUPS, MLOC = 32, 4, 4, 32
LINE = DEPTH * GROUPS
ROWS, LANES = 256, 128
PERIOD = 8192
MESH = pl.DeviceIdType.MESH


def split(table):
    high = table.astype(jnp.bfloat16)
    low = (table - high.astype(np.float32)).astype(jnp.bfloat16)
    return high, low


def tables():
    row = np.arange(ROWS)
    part, zl, plane = row // LANES, row // PLANE % DEPTH, row % PLANE
    index = plane // 2 * 8 + zl * 2 + plane % 2
    freq = np.arange(ROWS)
    angle = 2 * np.pi * (freq[:, None] * index[None, :] % ROWS) / ROWS
    cos, sin = np.cos(angle), np.sin(angle)
    first = np.concatenate(
        [np.where(part == 0, cos, sin), np.where(part == 0, -sin, cos)], 0
    )
    scale = 1.0 / (64 * PERIOD)
    last = scale * np.concatenate(
        [np.where(part == 0, sin, cos).T, np.where(part == 0, -cos, sin).T], 1
    )
    lane = np.arange(LANES)
    local, el = lane % MLOC, lane // MLOC
    same = (el[:, None] == el[None, :]).astype(np.float64)
    angle = 2 * np.pi * (local[:, None] * local[None, :] % MLOC) / MLOC
    cos, sin = same * np.cos(angle), same * np.sin(angle)
    middle = np.block([[cos, -sin], [sin, cos]])
    angle = 2 * np.pi * (freq[:, None] * local[None, :]) / PERIOD
    turn = np.stack([np.cos(angle), np.sin(angle)]).astype(np.float32)
    out = []
    for table in (first, middle, last):
        out.extend(split(table.astype(np.float32)))
    return [*out, turn]


def parts_of(x):
    high = x.astype(jnp.bfloat16)
    return high, (x - high.astype(jnp.float32)).astype(jnp.bfloat16)


def mm(a, b):
    return jnp.dot(a, b, preferred_element_type=jnp.float32)


def table_times(high, low, x):
    xh, xl = parts_of(x)
    return mm(high, xh) + (mm(high, xl) + mm(low, xh))


def times_table(x, high, low):
    xh, xl = parts_of(x)
    return mm(xh, high) + (mm(xl, high) + mm(xh, low))


def turned(real, imag, cos, sin):
    return real * cos + imag * sin, imag * cos - real * sin


def both(left, right):
    return jnp.concatenate([left, right], axis=1)


def correlate(a, b, f1h, f1l, f2h, f2l, gh, gl, turn):
    x = both(a, jnp.concatenate([b[:LANES], -b[LANES:]], 0))
    cos, sin = both(turn[0], turn[0]), both(turn[1], turn[1])
    y = table_times(f1h, f1l, x)
    yr, yi = turned(y[:ROWS], y[ROWS:], cos, sin)
    z = times_table(
        jnp.concatenate(
            [both(yr[:, :LANES], yi[:, :LANES]), both(yr[:, LANES:], yi[:, LANES:])], 0
        ),
        f2h,
        f2l,
    )
    ar, ai = z[:ROWS, :LANES], z[:ROWS, LANES:]
    br, bi = z[ROWS:, :LANES], z[ROWS:, LANES:]
    cr, ci = ar * br + ai * bi, ai * br - ar * bi
    v = times_table(jnp.concatenate([both(cr, ci), both(cr, -ci)], 0), f2h, f2l)
    er, ei = turned(
        both(v[:ROWS, :LANES], v[ROWS:, :LANES]),
        both(v[:ROWS, LANES:], v[ROWS:, LANES:]),
        cos,
        sin,
    )
    out = table_times(gh, gl, jnp.concatenate([er, ei], 0))
    q, p = out[:, :LANES], out[:, LANES:]
    return q, jnp.concatenate([-p[:LANES], p[LANES:]], 0)


def blocks_swapped(t):
    cut = [[t[32 * i : 32 * i + 32, 32 * j : 32 * j + 32] for j in range(4)] for i in range(4)]
    return [jnp.concatenate([cut[i][j] for i in range(4)], axis=1) for j in range(4)]


def to_owner(block, out):
    t = jnp.concatenate([block(zl) for zl in range(DEPTH)], 0).T
    for zl, rows in enumerate(blocks_swapped(t)):
        out[:, zl, :] = rows


def to_energies(got, store):
    rows = jnp.concatenate([got[:, zl, :] for zl in range(DEPTH)], 0)
    t = jnp.concatenate(blocks_swapped(rows), 0).T
    for zl in range(DEPTH):
        store(zl, t[MLOC * zl : MLOC * zl + MLOC])


def permute(src, dst, order):
    def tile(d, carry):
        at = jnp.broadcast_to(order[d], (8, LANES))
        lane, where = at % LANES, at // LANES
        total = jnp.zeros((8, LANES), jnp.float32)
        for s in range(LINE):
            moved = jnp.take_along_axis(src[:, s * LANES : (s + 1) * LANES], lane, axis=1)
            total = jnp.where(where == s, moved, total)
        dst[:, pl.ds(pl.multiple_of(d * LANES, LANES), LANES)] = total
        return carry

    lax.fori_loop(0, LINE, tile, 0)


def kernel(
    lesser, greater, partner, *refs,
):
    tables_in, refs = refs[:7], refs[7:]
    lesser_out, greater_out = refs[:2]
    tables_here, refs = refs[2:9], refs[9:]
    (
        order, z1, swapped, z2, zl_in, send_a, send_b, own_a, own_b,
        back_q, back_p, got_q, got_p, wide_q, wide_p, z2_back, unswapped,
        table_sem, sems, line_send, plane_send, few_send,
    ) = refs
    energy, zh = lax.axis_index("energy"), lax.axis_index("elem")
    w, zl = energy // 8 * 2 + energy % 2, energy // 2 % DEPTH
    z = zh * DEPTH + zl
    parts = (0, 1)

    def device(plane, low, high):
        return {"energy": plane // 2 * 8 + low * 2 + plane % 2, "elem": high}

    def line_peer(i):
        other = (z + LINE + (LINE // 2 - (i + 1) // 2) * (1 - 2 * (i % 2))) % LINE
        return other % DEPTH, other // DEPTH

    def far(t):
        return (54 >> (2 * t)) % 4

    def plane_peer(i):
        y = (w // 8 + far(i // 8)) % 4
        x = (w // 2 + far(i // 2 % 4)) % 4
        return y * 8 + x * 2 + (w + 1 + i) % 2

    def meet_zl(low):
        return (low + 2) % DEPTH

    def meet_zh(low, h):
        return (h + (low + 2) // DEPTH) % GROUPS

    def met_quarter(low, high):
        return (high + GROUPS - (3 - low) // 2) % GROUPS

    barrier = pltpu.get_barrier_semaphore()

    def greet_line(i, c):
        low, high = line_peer(i)
        pl.semaphore_signal(barrier, inc=1, device_id=device(w, low, high), device_id_type=MESH)
        return c

    def greet_plane(i, c):
        pl.semaphore_signal(
            barrier, inc=1, device_id=device(plane_peer(i), zl, zh), device_id_type=MESH
        )
        return c

    lax.fori_loop(0, LINE - 1, greet_line, 0)
    lax.fori_loop(0, PLANE - 1, greet_plane, 0)
    table_copies = [
        pltpu.make_async_copy(src, dst, table_sem.at[i])
        for i, (src, dst) in enumerate(zip(tables_in, tables_here))
    ]
    for copy in table_copies:
        copy.start()
    pl.semaphore_wait(barrier, LINE - 1 + PLANE - 1)

    def remote(src, dst, send, recv, where):
        return pltpu.make_async_remote_copy(
            src_ref=src, dst_ref=dst, send_sem=send, recv_sem=recv,
            device_id=where, device_id_type=MESH,
        )

    def arrived(whole, sem):
        pltpu.make_async_copy(whole, whole, sem).wait()

    def quarter(ref, part, h):
        return ref.at[part, pl.ds(pl.multiple_of(h * 8, 8), 8), :]

    def lanes(ref, start, size):
        return ref.at[..., pl.ds(pl.multiple_of(start, LANES), size)]

    started = []

    def send(phase, i, src, dst, recv, where):
        copy = remote(src, dst, few_send.at[phase, i], recv, where)
        copy.start()
        started.append(copy)

    def meet(phase, src, dst, recv):
        for i in range(GROUPS):
            h = (zh + 1 + i) % GROUPS
            send(phase, i, src(h), dst, recv, device(w, meet_zl(zl), meet_zh(zl, h)))

    def leave(phase, src, dst, recv):
        for i in range(GROUPS):
            h = (zh + 1 + i) % GROUPS
            send(phase, i, src(h), dst, recv, device(w, meet_zl(zl), h))

    def depths(phase, src, dst, recv):
        for i in range(DEPTH - 1):
            low = (zl + 1 + i) % DEPTH
            send(phase, i, src(low), dst, recv, device(w, low, zh))
        pltpu.make_async_copy(src(zl), dst, recv).start()

    def line_copy(phase, src, dst, recv, i):
        low, high = line_peer(i)
        return remote(src(low, high), dst, line_send.at[phase, i], recv, device(w, low, high))

    def line(phase, src, dst, recv):
        def start(i, c):
            line_copy(phase, src, dst, recv, i).start()
            return c

        lax.fori_loop(0, LINE - 1, start, 0)
        pltpu.make_async_copy(src(zl, zh), dst, recv).start()

    def line_done(phase, src, dst, recv):
        def done(i, c):
            line_copy(phase, src, dst, recv, i).wait_send()
            return c

        lax.fori_loop(0, LINE - 1, done, 0)

    def plane_copy(phase, src, dst, recv, i):
        other = plane_peer(i)
        return remote(
            src(other), dst(w), plane_send.at[phase, i], recv, device(other, zl, zh)
        )

    def plane(phase, src, dst, recv):
        def start(i, c):
            plane_copy(phase, src, dst, recv, i).start()
            return c

        lax.fori_loop(0, PLANE - 1, start, 0)
        pltpu.make_async_copy(src(w), dst(w), recv).start()

    def plane_done(phase, src, dst, recv):
        def done(i, c):
            plane_copy(phase, src, dst, recv, i).wait_send()
            return c

        lax.fori_loop(0, PLANE - 1, done, 0)

    def both_parts(ref):
        return lambda other: ref.at[:, other]

    def one_part(ref, part):
        return lambda other: ref.at[part, other]

    for i in range(GROUPS):
        h = (zh + 1 + i) % GROUPS
        send(0, i, partner, order.at[zh], sems.at[0], device(w, meet_zl(zl), h))
    for part in parts:
        meet(1 + part, lambda h: quarter(greater, part, h), lanes(z1.at[part], zh * 512, 512), sems.at[1 + part])
    depths(3, lambda low: lanes(lesser, low * LANES, LANES), zl_in.at[zl], sems.at[3])
    arrived(order, sems.at[0])
    flat = order.reshape(LINE, 1, LANES)

    def swapped_src(part):
        return lambda low, high: lanes(swapped.at[part], (high * DEPTH + low) * LANES, LANES)

    def z2_dst(part):
        return z2.at[part, meet_zl(zl), met_quarter(zl, zh)]

    for part in parts:
        arrived(z1.at[part], sems.at[1 + part])
        permute(z1.at[part], swapped.at[part], flat)
        line(part, swapped_src(part), z2_dst(part), sems.at[4 + part])
    arrived(zl_in, sems.at[3])
    for part in parts:
        to_owner(lambda low: zl_in[low, part], send_a.at[part])
    plane(0, both_parts(send_a), both_parts(own_a), sems.at[6])
    for part in parts:
        arrived(z2.at[part], sems.at[4 + part])
        to_owner(lambda low: z2[part, low].reshape(MLOC, LANES), send_b.at[part])
        plane(1 + part, one_part(send_b, part), one_part(own_b, part), sems.at[7 + part])
    arrived(own_a, sems.at[6])
    for part in parts:
        arrived(own_b.at[part], sems.at[7 + part])
    for copy in table_copies:
        copy.wait()

    def rows_of(ref):
        return jnp.concatenate([ref[part, :, low, :] for part in parts for low in range(DEPTH)], 0)

    def keep(ref, part, value):
        for low in range(DEPTH):
            ref[part, :, low, :] = value[part * LANES + low * PLANE : part * LANES + (low + 1) * PLANE]

    q, p = correlate(rows_of(own_a), rows_of(own_b), *[table[...] for table in tables_here])
    for part in parts:
        keep(back_q, part, q)
        plane(3 + part, one_part(back_q, part), one_part(got_q, part), sems.at[9 + part])
    for part in parts:
        keep(back_p, part, p)
    plane(5, both_parts(back_p), both_parts(got_p), sems.at[11])

    def wide_src(part):
        return lambda low, high: wide_q.at[part, meet_zl(low), met_quarter(low, high)]

    def back_dst(part):
        return lanes(z2_back.at[part], z * LANES, LANES)

    for part in parts:
        arrived(got_q.at[part], sems.at[9 + part])

        def keep_q(low, rows):
            wide_q[part, low] = rows.reshape(GROUPS, 8, LANES)

        to_energies(got_q.at[part], keep_q)
        line(2 + part, wide_src(part), back_dst(part), sems.at[12 + part])
    arrived(got_p, sems.at[11])
    for part in parts:

        def keep_p(low, rows):
            wide_p[low, part] = rows

        to_energies(got_p.at[part], keep_p)
    depths(4, lambda low: wide_p.at[low], lanes(lesser_out, zl * LANES, LANES), sems.at[14])
    for part in parts:
        arrived(z2_back.at[part], sems.at[12 + part])
        permute(z2_back.at[part], unswapped.at[part], flat)
        leave(
            5 + part,
            lambda h: lanes(unswapped.at[part], h * 512, 512),
            quarter(greater_out, part, met_quarter(zl, zh)),
            sems.at[15 + part],
        )
    arrived(lesser_out, sems.at[14])
    for part in parts:
        arrived(greater_out.at[part], sems.at[15 + part])
    for copy in started:
        copy.wait_send()
    plane_done(0, both_parts(send_a), both_parts(own_a), sems.at[6])
    plane_done(5, both_parts(back_p), both_parts(got_p), sems.at[11])
    for part in parts:
        line_done(part, swapped_src(part), z2_dst(part), sems.at[4 + part])
        line_done(2 + part, wide_src(part), back_dst(part), sems.at[12 + part])
        plane_done(1 + part, one_part(send_b, part), one_part(own_b, part), sems.at[7 + part])
        plane_done(3 + part, one_part(back_q, part), one_part(got_q, part), sems.at[9 + part])


def per_device(lesser, greater, partner):
    f32 = jnp.float32
    field = jax.ShapeDtypeStruct((2, MLOC, 512), f32)
    owned = pltpu.VMEM((2, PLANE, DEPTH, LANES), f32)
    long = pltpu.VMEM((2, 8, 2048), f32)
    deep = pltpu.VMEM((DEPTH, 2, MLOC, LANES), f32)
    cut = pltpu.VMEM((2, DEPTH, GROUPS, 8, LANES), f32)
    anywhere = pl.BlockSpec(memory_space=pl.ANY)
    constants = [jnp.asarray(table) for table in tables()]
    return pl.pallas_call(
        kernel,
        out_shape=(field, field),
        in_specs=[anywhere] * 10,
        out_specs=(anywhere, anywhere),
        scratch_shapes=[
            *[pltpu.VMEM(table.shape, table.dtype) for table in constants],
            pltpu.VMEM((GROUPS, 4, 1, LANES), jnp.int32),
            long, long, cut, deep, owned, owned, owned, owned,
            owned, owned, owned, owned, cut, deep, long, long,
            pltpu.SemaphoreType.DMA((7,)),
            pltpu.SemaphoreType.DMA((17,)),
            pltpu.SemaphoreType.DMA((4, LINE - 1)),
            pltpu.SemaphoreType.DMA((6, PLANE - 1)),
            pltpu.SemaphoreType.DMA((7, 4)),
        ],
        compiler_params=pltpu.CompilerParams(
            collective_id=0, has_side_effects=True, vmem_limit_bytes=48 * 1024 * 1024
        ),
    )(lesser, greater, partner.reshape(4, 1, LANES), *constants)


def solution(mesh):
    placed = (P(None, "energy", "elem"), P(None, "energy", "elem"), P("elem"))
    return jax.shard_map(
        per_device,
        mesh=mesh,
        in_specs=placed,
        out_specs=(P(None, "energy", "elem"), P(None, "energy", "elem")),
        check_vma=False,
    )
```

time: 92.7 us -> 83.5 us (0.901)
  the two profiles are of different devices: /device:TPU:1 before, /device:TPU:32 now
where the time goes in v1:
time: 83.5 us; the launch traced here: 83.1 us
  Pallas kernels  72.1 us (86%)
  local copies, waits for them, and re-layouts  10.4 us (12%)
    pallas_call x1, Pallas kernels, per_device(): pl.pallas_call(kernel, out_shape=(field, field), in_specs=[anywhere] * 10...  72.1 us
    unnamed x22, local copies, waits for them, and re-layouts  10.4 us

profile of v1, /device:TPU:32, one launch (start us, length us, event | category | flops | bytes accessed | tf_op | source)
XLA Modules:
  0.0 83.1 jit_solution(7058591820451462241)
XLA Ops:
  0.6 0.0 copy-start
  0.6 0.9 %copy-done = f32[2,256,128]{2,1,0:T(8,128)S(1)} copy-done((f32[2,256,128]{2,1,0:T(8,128)S(1)}, f32[2,256,128]{2,1,0:T(8,128)}, u32[]{:S(2)}) %copy-start) | copy-done | bytes 262168
  1.6 0.0 copy-start.1
  1.6 0.9 %copy-done.1 = bf16[256,512]{1,0:T(8,128)(2,1)S(1)} copy-done((bf16[256,512]{1,0:T(8,128)(2,1)S(1)}, bf16[256,512]{1,0:T(8,128)(2,1)}, u32[]{:S(2)}) %copy-start.1) | copy-done | bytes 262168
  2.5 0.0 copy-start.2
  2.5 0.9 %copy-done.2 = bf16[256,512]{1,0:T(8,128)(2,1)S(1)} copy-done((bf16[256,512]{1,0:T(8,128)(2,1)S(1)}, bf16[256,512]{1,0:T(8,128)(2,1)}, u32[]{:S(2)}) %copy-start.2) | copy-done | bytes 262168
  3.5 0.0 copy-start.3
  3.5 0.9 %copy-done.3 = bf16[512,256]{1,0:T(8,128)(2,1)S(1)} copy-done((bf16[512,256]{1,0:T(8,128)(2,1)S(1)}, bf16[512,256]{1,0:T(8,128)(2,1)}, u32[]{:S(2)}) %copy-start.3) | copy-done | bytes 262168
  4.4 0.0 copy-start.4
  4.4 0.9 %copy-done.4 = bf16[512,256]{1,0:T(8,128)(2,1)S(1)} copy-done((bf16[512,256]{1,0:T(8,128)(2,1)S(1)}, bf16[512,256]{1,0:T(8,128)(2,1)}, u32[]{:S(2)}) %copy-start.4) | copy-done | bytes 262168
  5.4 0.0 copy-start.5
  5.4 0.9 %copy-done.5 = f32[2,32,512]{2,1,0:T(8,128)S(1)} copy-done((f32[2,32,512]{2,1,0:T(8,128)S(1)}, f32[2,32,512]{2,1,0:T(8,128)}, u32[]{:S(2)}) %copy-start.5) | copy-done | bytes 131096
  6.3 0.0 copy-start.6
  6.3 0.9 %copy-done.6 = f32[2,32,512]{2,1,0:T(8,128)S(1)} copy-done((f32[2,32,512]{2,1,0:T(8,128)S(1)}, f32[2,32,512]{2,1,0:T(8,128)}, u32[]{:S(2)}) %copy-start.6) | copy-done | bytes 131096
  7.2 0.0 copy-start.7
  7.2 0.9 %copy-done.7 = bf16[256,256]{1,0:T(8,128)(2,1)S(1)} copy-done((bf16[256,256]{1,0:T(8,128)(2,1)S(1)}, bf16[256,256]{1,0:T(8,128)(2,1)}, u32[]{:S(2)}) %copy-start.7) | copy-done | bytes 131096
  8.1 0.0 copy-start.8
  8.1 0.9 %copy-done.8 = bf16[256,256]{1,0:T(8,128)(2,1)S(1)} copy-done((bf16[256,256]{1,0:T(8,128)(2,1)S(1)}, bf16[256,256]{1,0:T(8,128)(2,1)}, u32[]{:S(2)}) %copy-start.8) | copy-done | bytes 131096
  9.0 0.0 copy-start.9
  9.0 0.7 copy-done.9
  9.7 72.1 %shard_map.113 = (f32[2,32,512]{2,1,0:T(8,128)S(1)}, f32[2,32,512]{2,1,0:T(8,128)S(1)}) custom-call(f32[2,32,512]{2,1,0:T(8,128)S(1)} %copy-done.5, f32[2,32,512]{2,1,0:T(8,128)S(1)} %copy-done.6, s32[4,1,128]{2,1,0:T(1,128)S(1)} %bitcast.1, bf16[512,256]{1,0:T(8,128)(2,1)S(1)} %copy-done.4, bf16[512,256]{1,0:T(8,128)(2,1)S(1)} %copy-done.3, ...), custom_call_target="tpu_custom_call" | custom-call | tf_op jit(solution)/shard_map/pallas_call | solution.py:385
  81.8 0.7 copy.14
  82.5 0.7 copy.15
Async XLA Ops:
  0.6 1.0 %copy-start = (f32[2,256,128]{2,1,0:T(8,128)S(1)}, f32[2,256,128]{2,1,0:T(8,128)}, u32[]{:S(2)}) copy-start(f32[2,256,128]{2,1,0:T(8,128)} %constant.20.clone.refs_6_) | copy-start | bytes 786436
  1.6 0.9 %copy-start.1 = (bf16[256,512]{1,0:T(8,128)(2,1)S(1)}, bf16[256,512]{1,0:T(8,128)(2,1)}, u32[]{:S(2)}) copy-start(bf16[256,512]{1,0:T(8,128)(2,1)} %constant.19.clone.refs_5_) | copy-start | bytes 786436
  2.5 0.9 %copy-start.2 = (bf16[256,512]{1,0:T(8,128)(2,1)S(1)}, bf16[256,512]{1,0:T(8,128)(2,1)}, u32[]{:S(2)}) copy-start(bf16[256,512]{1,0:T(8,128)(2,1)} %constant.18.clone.refs_4_) | copy-start | bytes 786436
  3.5 0.9 %copy-start.3 = (bf16[512,256]{1,0:T(8,128)(2,1)S(1)}, bf16[512,256]{1,0:T(8,128)(2,1)}, u32[]{:S(2)}) copy-start(bf16[512,256]{1,0:T(8,128)(2,1)} %constant.15.clone.refs_1_) | copy-start | bytes 786436
  4.4 0.9 %copy-start.4 = (bf16[512,256]{1,0:T(8,128)(2,1)S(1)}, bf16[512,256]{1,0:T(8,128)(2,1)}, u32[]{:S(2)}) copy-start(bf16[512,256]{1,0:T(8,128)(2,1)} %constant.14.clone.refs_0_) | copy-start | bytes 786436
  5.4 0.9 %copy-start.5 = (f32[2,32,512]{2,1,0:T(8,128)S(1)}, f32[2,32,512]{2,1,0:T(8,128)}, u32[]{:S(2)}) copy-start(f32[2,32,512]{2,1,0:T(8,128)} %lesser.1) | copy-start | bytes 393220
  6.3 0.9 %copy-start.6 = (f32[2,32,512]{2,1,0:T(8,128)S(1)}, f32[2,32,512]{2,1,0:T(8,128)}, u32[]{:S(2)}) copy-start(f32[2,32,512]{2,1,0:T(8,128)} %greater.1) | copy-start | bytes 393220
  7.2 0.9 %copy-start.7 = (bf16[256,256]{1,0:T(8,128)(2,1)S(1)}, bf16[256,256]{1,0:T(8,128)(2,1)}, u32[]{:S(2)}) copy-start(bf16[256,256]{1,0:T(8,128)(2,1)} %constant.17.clone.refs_3_) | copy-start | bytes 393220
  8.1 0.9 %copy-start.8 = (bf16[256,256]{1,0:T(8,128)(2,1)S(1)}, bf16[256,256]{1,0:T(8,128)(2,1)}, u32[]{:S(2)}) copy-start(bf16[256,256]{1,0:T(8,128)(2,1)} %constant.16.clone.refs_2_) | copy-start | bytes 393220
  9.0 0.7 copy-start.9

commit v2 on v1

--- a/solution.py
+++ b/solution.py
@@ -11,12 +11,6 @@
 ROWS, LANES = 256, 128
 PERIOD = 8192
 MESH = pl.DeviceIdType.MESH
-
-
-def split(table):
-    high = table.astype(jnp.bfloat16)
-    low = (table - high.astype(np.float32)).astype(jnp.bfloat16)
-    return high, low
 
 
 def tables():
@@ -41,10 +35,7 @@
     middle = np.block([[cos, -sin], [sin, cos]])
     angle = 2 * np.pi * (freq[:, None] * local[None, :]) / PERIOD
     turn = np.stack([np.cos(angle), np.sin(angle)]).astype(np.float32)
-    out = []
-    for table in (first, middle, last):
-        out.extend(split(table.astype(np.float32)))
-    return [*out, turn]
+    return [*(table.astype(np.float32) for table in (first, middle, last)), turn]
 
 
 def parts_of(x):
@@ -56,12 +47,14 @@
     return jnp.dot(a, b, preferred_element_type=jnp.float32)
 
 
-def table_times(high, low, x):
+def table_times(table, x):
+    high, low = table
     xh, xl = parts_of(x)
     return mm(high, xh) + (mm(high, xl) + mm(low, xh))
 
 
-def times_table(x, high, low):
+def times_table(x, table):
+    high, low = table
     xh, xl = parts_of(x)
     return mm(xh, high) + (mm(xl, high) + mm(xh, low))
 
@@ -74,29 +67,28 @@
     return jnp.concatenate([left, right], axis=1)
 
 
-def correlate(a, b, f1h, f1l, f2h, f2l, gh, gl, turn):
+def correlate(a, b, first, middle, last, turn):
     x = both(a, jnp.concatenate([b[:LANES], -b[LANES:]], 0))
     cos, sin = both(turn[0], turn[0]), both(turn[1], turn[1])
-    y = table_times(f1h, f1l, x)
+    y = table_times(first, x)
     yr, yi = turned(y[:ROWS], y[ROWS:], cos, sin)
     z = times_table(
         jnp.concatenate(
             [both(yr[:, :LANES], yi[:, :LANES]), both(yr[:, LANES:], yi[:, LANES:])], 0
         ),
-        f2h,
-        f2l,
+        middle,
     )
     ar, ai = z[:ROWS, :LANES], z[:ROWS, LANES:]
     br, bi = z[ROWS:, :LANES], z[ROWS:, LANES:]
     cr, ci = ar * br + ai * bi, ai * br - ar * bi
-    v = times_table(jnp.concatenate([both(cr, ci), both(cr, -ci)], 0), f2h, f2l)
+    v = times_table(jnp.concatenate([both(cr, ci), both(cr, -ci)], 0), middle)
     er, ei = turned(
         both(v[:ROWS, :LANES], v[ROWS:, :LANES]),
         both(v[:ROWS, LANES:], v[ROWS:, LANES:]),
         cos,
         sin,
     )
-    out = table_times(gh, gl, jnp.concatenate([er, ei], 0))
+    out = table_times(last, jnp.concatenate([er, ei], 0))
     q, p = out[:, :LANES], out[:, LANES:]
     return q, jnp.concatenate([-p[:LANES], p[LANES:]], 0)
 
@@ -136,9 +128,9 @@
 def kernel(
     lesser, greater, partner, *refs,
 ):
-    tables_in, refs = refs[:7], refs[7:]
+    tables_in, refs = refs[:4], refs[4:]
     lesser_out, greater_out = refs[:2]
-    tables_here, refs = refs[2:9], refs[9:]
+    tables_here, halves, refs = refs[2:6], refs[6:9], refs[9:]
     (
         order, z1, swapped, z2, zl_in, send_a, send_b, own_a, own_b,
         back_q, back_p, got_q, got_p, wide_q, wide_p, z2_back, unswapped,
@@ -299,6 +291,10 @@
         arrived(z1.at[part], sems.at[1 + part])
         permute(z1.at[part], swapped.at[part], flat)
         line(part, swapped_src(part), z2_dst(part), sems.at[4 + part])
+    for copy in table_copies:
+        copy.wait()
+    for table, half in zip(tables_here, halves):
+        half[0], half[1] = parts_of(table[...])
     arrived(zl_in, sems.at[3])
     for part in parts:
         to_owner(lambda low: zl_in[low, part], send_a.at[part])
@@ -310,8 +306,6 @@
     arrived(own_a, sems.at[6])
     for part in parts:
         arrived(own_b.at[part], sems.at[7 + part])
-    for copy in table_copies:
-        copy.wait()
 
     def rows_of(ref):
         return jnp.concatenate([ref[part, :, low, :] for part in parts for low in range(DEPTH)], 0)
@@ -320,7 +314,9 @@
         for low in range(DEPTH):
             ref[part, :, low, :] = value[part * LANES + low * PLANE : part * LANES + (low + 1) * PLANE]
 
-    q, p = correlate(rows_of(own_a), rows_of(own_b), *[table[...] for table in tables_here])
+    q, p = correlate(
+        rows_of(own_a), rows_of(own_b), *[(half[0], half[1]) for half in halves], tables_here[3]
+    )
     for part in parts:
         keep(back_q, part, q)
         plane(3 + part, one_part(back_q, part), one_part(got_q, part), sems.at[9 + part])
@@ -380,26 +376,27 @@
     long = pltpu.VMEM((2, 8, 2048), f32)
     deep = pltpu.VMEM((DEPTH, 2, MLOC, LANES), f32)
     cut = pltpu.VMEM((2, DEPTH, GROUPS, 8, LANES), f32)
-    anywhere = pl.BlockSpec(memory_space=pl.ANY)
+    anywhere = pl.BlockSpec(memory_space=pltpu.HBM)
     constants = [jnp.asarray(table) for table in tables()]
     return pl.pallas_call(
         kernel,
         out_shape=(field, field),
-        in_specs=[anywhere] * 10,
+        in_specs=[anywhere] * 7,
         out_specs=(anywhere, anywhere),
         scratch_shapes=[
             *[pltpu.VMEM(table.shape, table.dtype) for table in constants],
+            *[pltpu.VMEM((2, *table.shape), jnp.bfloat16) for table in constants[:3]],
             pltpu.VMEM((GROUPS, 4, 1, LANES), jnp.int32),
             long, long, cut, deep, owned, owned, owned, owned,
             owned, owned, owned, owned, cut, deep, long, long,
-            pltpu.SemaphoreType.DMA((7,)),
+            pltpu.SemaphoreType.DMA((4,)),
             pltpu.SemaphoreType.DMA((17,)),
             pltpu.SemaphoreType.DMA((4, LINE - 1)),
             pltpu.SemaphoreType.DMA((6, PLANE - 1)),
             pltpu.SemaphoreType.DMA((7, 4)),
         ],
         compiler_params=pltpu.CompilerParams(
-            collective_id=0, has_side_effects=True, vmem_limit_bytes=48 * 1024 * 1024
+            collective_id=0, has_side_effects=True, vmem_limit_bytes=56 * 1024 * 1024
         ),
     )(lesser, greater, partner.reshape(4, 1, LANES), *constants)
 

time: 83.5 us -> 75.5 us (0.904)
  the two profiles are of different devices: /device:TPU:32 before, /device:TPU:1 now
where the time goes in v2:
time: 75.5 us; the launch traced here: 74 us
  Pallas kernels  71.1 us (94%)
  local copies, waits for them, and re-layouts  2.26 us (3%)
    pallas_call x1, Pallas kernels, per_device(): pl.pallas_call(kernel, out_shape=(field, field), in_specs=[anywhere] * 7,...  71.1 us
    unnamed x4, local copies, waits for them, and re-layouts  2.26 us

profile of v2, /device:TPU:1, one launch (start us, length us, event | category | flops | bytes accessed | tf_op | source)
XLA Modules:
  0.0 74.0 jit_solution(6022083474400391234)
XLA Ops:
  0.6 71.1 %shard_map.86 = (f32[2,32,512]{2,1,0:T(8,128)}, f32[2,32,512]{2,1,0:T(8,128)}) custom-call(f32[2,32,512]{2,1,0:T(8,128)} %lesser.1, f32[2,32,512]{2,1,0:T(8,128)} %greater.1, s32[4,1,128]{2,1,0:T(1,128)} %bitcast.1, f32[512,256]{1,0:T(8,128)} %constant.8.clone.refs_0_, f32[256,256]{1,0:T(8,128)} %constant.9.clone.refs_1_, ...), custom_call_target="tpu_custom_call" | custom-call | tf_op jit(solution)/shard_map/pallas_call | solution.py:381
  71.7 0.0 copy-start
  71.8 1.6 %copy.11 = f32[2,32,512]{2,1,0:T(8,128)} copy(f32[2,32,512]{2,1,0:T(8,128)} %get-tuple-element.4) | data formatting | bytes 262144
  73.4 0.0 copy-done
  73.4 0.7 copy.12
Async XLA Ops:
  71.7 1.6 %copy-start = (f32[2,32,512]{2,1,0:T(8,128)S(1)}, f32[2,32,512]{2,1,0:T(8,128)}, u32[]{:S(2)}) copy-start(f32[2,32,512]{2,1,0:T(8,128)} %get-tuple-element.5) | copy-start | bytes 393220

commit v3 on v2

--- a/solution.py
+++ b/solution.py
@@ -67,30 +67,23 @@
     return jnp.concatenate([left, right], axis=1)
 
 
-def correlate(a, b, first, middle, last, turn):
-    x = both(a, jnp.concatenate([b[:LANES], -b[LANES:]], 0))
-    cos, sin = both(turn[0], turn[0]), both(turn[1], turn[1])
-    y = table_times(first, x)
-    yr, yi = turned(y[:ROWS], y[ROWS:], cos, sin)
-    z = times_table(
-        jnp.concatenate(
-            [both(yr[:, :LANES], yi[:, :LANES]), both(yr[:, LANES:], yi[:, LANES:])], 0
-        ),
-        middle,
-    )
-    ar, ai = z[:ROWS, :LANES], z[:ROWS, LANES:]
-    br, bi = z[ROWS:, :LANES], z[ROWS:, LANES:]
-    cr, ci = ar * br + ai * bi, ai * br - ar * bi
-    v = times_table(jnp.concatenate([both(cr, ci), both(cr, -ci)], 0), middle)
-    er, ei = turned(
-        both(v[:ROWS, :LANES], v[ROWS:, :LANES]),
-        both(v[:ROWS, LANES:], v[ROWS:, LANES:]),
-        cos,
-        sin,
-    )
-    out = table_times(last, jnp.concatenate([er, ei], 0))
-    q, p = out[:, :LANES], out[:, LANES:]
-    return q, jnp.concatenate([-p[:LANES], p[LANES:]], 0)
+def forward(rows, first, middle, cos, sin):
+    y = table_times(first, rows)
+    return times_table(both(*turned(y[:ROWS], y[ROWS:], cos, sin)), middle)
+
+
+def conjugate(z):
+    return both(z[:, :LANES], -z[:, LANES:])
+
+
+def product(a, b):
+    ar, ai, br, bi = a[:, :LANES], a[:, LANES:], b[:, :LANES], b[:, LANES:]
+    return both(ar * br + ai * bi, ai * br - ar * bi)
+
+
+def inverse(z, middle, last, cos, sin):
+    v = times_table(z, middle)
+    return table_times(last, jnp.concatenate(turned(v[:, :LANES], v[:, LANES:], cos, sin), 0))
 
 
 def blocks_swapped(t):
@@ -111,18 +104,14 @@
         store(zl, t[MLOC * zl : MLOC * zl + MLOC])
 
 
-def permute(src, dst, order):
-    def tile(d, carry):
-        at = jnp.broadcast_to(order[d], (8, LANES))
-        lane, where = at % LANES, at // LANES
-        total = jnp.zeros((8, LANES), jnp.float32)
-        for s in range(LINE):
-            moved = jnp.take_along_axis(src[:, s * LANES : (s + 1) * LANES], lane, axis=1)
-            total = jnp.where(where == s, moved, total)
-        dst[:, pl.ds(pl.multiple_of(d * LANES, LANES), LANES)] = total
-        return carry
-
-    lax.fori_loop(0, LINE, tile, 0)
+def permuted(src, order, d):
+    at = jnp.broadcast_to(order[d], (8, LANES))
+    lane, where = at % LANES, at // LANES
+    total = jnp.take_along_axis(src[:, :LANES], lane, axis=1)
+    for s in range(1, LINE):
+        moved = jnp.take_along_axis(src[:, s * LANES : (s + 1) * LANES], lane, axis=1)
+        total = jnp.where(where == s, moved, total)
+    return total
 
 
 def kernel(
@@ -132,8 +121,8 @@
     lesser_out, greater_out = refs[:2]
     tables_here, halves, refs = refs[2:6], refs[6:9], refs[9:]
     (
-        order, z1, swapped, z2, zl_in, send_a, send_b, own_a, own_b,
-        back_q, back_p, got_q, got_p, wide_q, wide_p, z2_back, unswapped,
+        order, z1, swapped, z2, lesser_here, send_a, mid_a, deep_a, own_a, freq_a, send_b, own_b,
+        back_q, got_q, wide_q, z2_back, unswapped, freq_p, back_p, mid_p, send_p, got_p, lesser_done,
         table_sem, sems, line_send, plane_send, few_send,
     ) = refs
     energy, zh = lax.axis_index("energy"), lax.axis_index("elem")
@@ -186,6 +175,11 @@
     ]
     for copy in table_copies:
         copy.start()
+    lesser_copy = pltpu.make_async_copy(lesser, lesser_here, table_sem.at[4])
+    lesser_copy.start()
+    lesser_copy.wait()
+    for part in parts:
+        to_owner(lambda low: lesser_here[part, :, low * LANES : (low + 1) * LANES], send_a.at[part])
     pl.semaphore_wait(barrier, LINE - 1 + PLANE - 1)
 
     def remote(src, dst, send, recv, where):
@@ -215,11 +209,6 @@
             h = (zh + 1 + i) % GROUPS
             send(phase, i, src(h), dst, recv, device(w, meet_zl(zl), meet_zh(zl, h)))
 
-    def leave(phase, src, dst, recv):
-        for i in range(GROUPS):
-            h = (zh + 1 + i) % GROUPS
-            send(phase, i, src(h), dst, recv, device(w, meet_zl(zl), h))
-
     def depths(phase, src, dst, recv):
         for i in range(DEPTH - 1):
             low = (zl + 1 + i) % DEPTH
@@ -230,12 +219,16 @@
         low, high = line_peer(i)
         return remote(src(low, high), dst, line_send.at[phase, i], recv, device(w, low, high))
 
-    def line(phase, src, dst, recv):
+    def line(phase, src, dst, recv, make=None):
         def start(i, c):
+            if make is not None:
+                make(*line_peer(i))
             line_copy(phase, src, dst, recv, i).start()
             return c
 
-        lax.fori_loop(0, LINE - 1, start, 0)
+        lax.fori_loop(0, LINE - 1, start, 0, unroll=3)
+        if make is not None:
+            make(zl, zh)
         pltpu.make_async_copy(src(zl, zh), dst, recv).start()
 
     def line_done(phase, src, dst, recv):
@@ -256,7 +249,7 @@
             plane_copy(phase, src, dst, recv, i).start()
             return c
 
-        lax.fori_loop(0, PLANE - 1, start, 0)
+        lax.fori_loop(0, PLANE - 1, start, 0, unroll=4)
         pltpu.make_async_copy(src(w), dst(w), recv).start()
 
     def plane_done(phase, src, dst, recv):
@@ -272,57 +265,65 @@
     def one_part(ref, part):
         return lambda other: ref.at[part, other]
 
+    def make_tile(src, dst):
+        def make(low, high):
+            d = high * DEPTH + low
+            dst[:, pl.ds(pl.multiple_of(d * LANES, LANES), LANES)] = permuted(src, flat, d)
+
+        return make
+
     for i in range(GROUPS):
         h = (zh + 1 + i) % GROUPS
         send(0, i, partner, order.at[zh], sems.at[0], device(w, meet_zl(zl), h))
     for part in parts:
         meet(1 + part, lambda h: quarter(greater, part, h), lanes(z1.at[part], zh * 512, 512), sems.at[1 + part])
-    depths(3, lambda low: lanes(lesser, low * LANES, LANES), zl_in.at[zl], sems.at[3])
-    arrived(order, sems.at[0])
-    flat = order.reshape(LINE, 1, LANES)
-
-    def swapped_src(part):
-        return lambda low, high: lanes(swapped.at[part], (high * DEPTH + low) * LANES, LANES)
-
-    def z2_dst(part):
-        return z2.at[part, meet_zl(zl), met_quarter(zl, zh)]
-
-    for part in parts:
-        arrived(z1.at[part], sems.at[1 + part])
-        permute(z1.at[part], swapped.at[part], flat)
-        line(part, swapped_src(part), z2_dst(part), sems.at[4 + part])
+    plane(0, both_parts(send_a), both_parts(mid_a), sems.at[6])
     for copy in table_copies:
         copy.wait()
     for table, half in zip(tables_here, halves):
         half[0], half[1] = parts_of(table[...])
-    arrived(zl_in, sems.at[3])
-    for part in parts:
-        to_owner(lambda low: zl_in[low, part], send_a.at[part])
-    plane(0, both_parts(send_a), both_parts(own_a), sems.at[6])
+    first, middle, last = [lambda half=half: (half[0], half[1]) for half in halves]
+    turn = tables_here[3]
+    arrived(order, sems.at[0])
+    flat = order.reshape(LINE, 1, LANES)
+
+    def swapped_src(part):
+        return lambda low, high: lanes(swapped.at[part], (high * DEPTH + low) * LANES, LANES)
+
+    def z2_dst(part):
+        return z2.at[part, meet_zl(zl), met_quarter(zl, zh)]
+
+    for part in parts:
+        arrived(z1.at[part], sems.at[1 + part])
+        line(part, swapped_src(part), z2_dst(part), sems.at[4 + part], make_tile(z1.at[part], swapped.at[part]))
+    arrived(mid_a, sems.at[6])
+    for low in range(DEPTH):
+        for part in parts:
+            deep_a[low, part] = mid_a[part, :, low, :]
+    depths(3, lambda low: deep_a.at[low], own_a.at[:, zl], sems.at[3])
     for part in parts:
         arrived(z2.at[part], sems.at[4 + part])
         to_owner(lambda low: z2[part, low].reshape(MLOC, LANES), send_b.at[part])
         plane(1 + part, one_part(send_b, part), one_part(own_b, part), sems.at[7 + part])
-    arrived(own_a, sems.at[6])
+    arrived(own_a, sems.at[3])
+    freq_a[...] = forward(own_a[...].reshape(ROWS, LANES), first(), middle(), turn[0], turn[1])
     for part in parts:
         arrived(own_b.at[part], sems.at[7 + part])
-
-    def rows_of(ref):
-        return jnp.concatenate([ref[part, :, low, :] for part in parts for low in range(DEPTH)], 0)
-
-    def keep(ref, part, value):
+    rows_b = jnp.concatenate(
+        [(own_b[part, :, low, :] if part == 0 else -own_b[part, :, low, :]) for part in parts for low in range(DEPTH)], 0
+    )
+    joint = product(freq_a[...], forward(rows_b, first(), middle(), turn[0], turn[1]))
+    freq_p[...] = conjugate(joint)
+    q = inverse(joint, middle(), last(), turn[0], turn[1])
+    for part in parts:
         for low in range(DEPTH):
-            ref[part, :, low, :] = value[part * LANES + low * PLANE : part * LANES + (low + 1) * PLANE]
-
-    q, p = correlate(
-        rows_of(own_a), rows_of(own_b), *[(half[0], half[1]) for half in halves], tables_here[3]
-    )
-    for part in parts:
-        keep(back_q, part, q)
+            back_q[part, :, low, :] = q[part * LANES + low * PLANE : part * LANES + (low + 1) * PLANE]
         plane(3 + part, one_part(back_q, part), one_part(got_q, part), sems.at[9 + part])
-    for part in parts:
-        keep(back_p, part, p)
-    plane(5, both_parts(back_p), both_parts(got_p), sems.at[11])
+    p = inverse(freq_p[...], middle(), last(), turn[0], turn[1])
+    for low in range(DEPTH):
+        back_p[low, 0] = -p[low * PLANE : (low + 1) * PLANE]
+        back_p[low, 1] = p[LANES + low * PLANE : LANES + (low + 1) * PLANE]
+    depths(4, lambda low: back_p.at[low], mid_p.at[:, zl], sems.at[14])
 
     def wide_src(part):
         return lambda low, high: wide_q.at[part, meet_zl(low), met_quarter(low, high)]
@@ -338,35 +339,44 @@
 
         to_energies(got_q.at[part], keep_q)
         line(2 + part, wide_src(part), back_dst(part), sems.at[12 + part])
+    arrived(mid_p, sems.at[14])
+    for part in parts:
+        for low in range(DEPTH):
+            send_p[part, :, low, :] = mid_p[part, low]
+    plane(5, both_parts(send_p), both_parts(got_p), sems.at[11])
+    for part in parts:
+        arrived(z2_back.at[part], sems.at[12 + part])
+        make = make_tile(z2_back.at[part], unswapped.at[part])
+        for i in range(GROUPS):
+            h = (zh + 1 + i) % GROUPS
+            for low in range(DEPTH):
+                make(low, h)
+            send(
+                5 + part, i, lanes(unswapped.at[part], h * 512, 512),
+                quarter(greater_out, part, met_quarter(zl, zh)), sems.at[15 + part],
+                device(w, meet_zl(zl), h),
+            )
     arrived(got_p, sems.at[11])
     for part in parts:
 
         def keep_p(low, rows):
-            wide_p[low, part] = rows
+            lesser_done[part, :, low * LANES : (low + 1) * LANES] = rows
 
         to_energies(got_p.at[part], keep_p)
-    depths(4, lambda low: wide_p.at[low], lanes(lesser_out, zl * LANES, LANES), sems.at[14])
-    for part in parts:
-        arrived(z2_back.at[part], sems.at[12 + part])
-        permute(z2_back.at[part], unswapped.at[part], flat)
-        leave(
-            5 + part,
-            lambda h: lanes(unswapped.at[part], h * 512, 512),
-            quarter(greater_out, part, met_quarter(zl, zh)),
-            sems.at[15 + part],
-        )
-    arrived(lesser_out, sems.at[14])
-    for part in parts:
-        arrived(greater_out.at[part], sems.at[15 + part])
+    lesser_copy = pltpu.make_async_copy(lesser_done, lesser_out, table_sem.at[5])
+    lesser_copy.start()
     for copy in started:
         copy.wait_send()
-    plane_done(0, both_parts(send_a), both_parts(own_a), sems.at[6])
-    plane_done(5, both_parts(back_p), both_parts(got_p), sems.at[11])
+    plane_done(0, both_parts(send_a), both_parts(mid_a), sems.at[6])
+    plane_done(5, both_parts(send_p), both_parts(got_p), sems.at[11])
     for part in parts:
         line_done(part, swapped_src(part), z2_dst(part), sems.at[4 + part])
         line_done(2 + part, wide_src(part), back_dst(part), sems.at[12 + part])
         plane_done(1 + part, one_part(send_b, part), one_part(own_b, part), sems.at[7 + part])
         plane_done(3 + part, one_part(back_q, part), one_part(got_q, part), sems.at[9 + part])
+    lesser_copy.wait()
+    for part in parts:
+        arrived(greater_out.at[part], sems.at[15 + part])
 
 
 def per_device(lesser, greater, partner):
@@ -374,7 +384,10 @@
     field = jax.ShapeDtypeStruct((2, MLOC, 512), f32)
     owned = pltpu.VMEM((2, PLANE, DEPTH, LANES), f32)
     long = pltpu.VMEM((2, 8, 2048), f32)
-    deep = pltpu.VMEM((DEPTH, 2, MLOC, LANES), f32)
+    whole = pltpu.VMEM((2, MLOC, 512), f32)
+    deep = pltpu.VMEM((DEPTH, 2, PLANE, LANES), f32)
+    sorted_ = pltpu.VMEM((2, DEPTH, PLANE, LANES), f32)
+    freq = pltpu.VMEM((ROWS, ROWS), f32)
     cut = pltpu.VMEM((2, DEPTH, GROUPS, 8, LANES), f32)
     anywhere = pl.BlockSpec(memory_space=pltpu.HBM)
     constants = [jnp.asarray(table) for table in tables()]
@@ -387,9 +400,9 @@
             *[pltpu.VMEM(table.shape, table.dtype) for table in constants],
             *[pltpu.VMEM((2, *table.shape), jnp.bfloat16) for table in constants[:3]],
             pltpu.VMEM((GROUPS, 4, 1, LANES), jnp.int32),
-            long, long, cut, deep, owned, owned, owned, owned,
-            owned, owned, owned, owned, cut, deep, long, long,
-            pltpu.SemaphoreType.DMA((4,)),
+            long, long, cut, whole, owned, owned, deep, sorted_, freq, owned, owned,
+            owned, owned, cut, long, long, freq, deep, sorted_, owned, owned, whole,
+            pltpu.SemaphoreType.DMA((6,)),
             pltpu.SemaphoreType.DMA((17,)),
             pltpu.SemaphoreType.DMA((4, LINE - 1)),
             pltpu.SemaphoreType.DMA((6, PLANE - 1)),

time: 75.5 us -> 70.6 us (0.935)
  the two profiles are of different devices: /device:TPU:1 before, /device:TPU:32 now
where the time goes in v3:
time: 70.6 us; the launch traced here: 70.5 us
  Pallas kernels  67.6 us (96%)
  local copies, waits for them, and re-layouts  2.26 us (3%)
    pallas_call x1, Pallas kernels, per_device(): pl.pallas_call(kernel, out_shape=(field, field), in_specs=[anywhere] * 7,...  67.6 us
    unnamed x4, local copies, waits for them, and re-layouts  2.26 us

profile of v3, /device:TPU:32, one launch (start us, length us, event | category | flops | bytes accessed | tf_op | source)
XLA Modules:
  0.0 70.5 jit_solution(9228728242220659025)
XLA Ops:
  0.6 67.6 %shard_map.86 = (f32[2,32,512]{2,1,0:T(8,128)}, f32[2,32,512]{2,1,0:T(8,128)}) custom-call(f32[2,32,512]{2,1,0:T(8,128)} %lesser.1, f32[2,32,512]{2,1,0:T(8,128)} %greater.1, s32[4,1,128]{2,1,0:T(1,128)} %bitcast.1, f32[512,256]{1,0:T(8,128)} %constant.8.clone.refs_0_, f32[256,256]{1,0:T(8,128)} %constant.9.clone.refs_1_, ...), custom_call_target="tpu_custom_call" | custom-call | tf_op jit(solution)/shard_map/pallas_call | solution.py:394
  68.2 0.0 copy-start
  68.2 1.6 %copy.11 = f32[2,32,512]{2,1,0:T(8,128)} copy(f32[2,32,512]{2,1,0:T(8,128)} %get-tuple-element.4) | data formatting | bytes 262144
  69.8 0.0 copy-done
  69.8 0.7 copy.12
Async XLA Ops:
  68.2 1.6 %copy-start = (f32[2,32,512]{2,1,0:T(8,128)S(1)}, f32[2,32,512]{2,1,0:T(8,128)}, u32[]{:S(2)}) copy-start(f32[2,32,512]{2,1,0:T(8,128)} %get-tuple-element.5) | copy-start | bytes 393220

commit v4 on v3

--- a/solution.py
+++ b/solution.py
@@ -11,6 +11,9 @@
 ROWS, LANES = 256, 128
 PERIOD = 8192
 MESH = pl.DeviceIdType.MESH
+HOPS = (0, 1, 2, 1)
+PLANE_STEPS = sorted(range(1, PLANE), key=lambda k: -HOPS[k >> 3] - HOPS[k >> 1 & 3])
+LINE_STEPS = (8, 9, 10, 11, 7, 6, 14, 13, 5, 12, 4, 15, 3, 2, 1)
 
 
 def tables():
@@ -137,13 +140,26 @@
         other = (z + LINE + (LINE // 2 - (i + 1) // 2) * (1 - 2 * (i % 2))) % LINE
         return other % DEPTH, other // DEPTH
 
-    def far(t):
-        return (54 >> (2 * t)) % 4
-
-    def plane_peer(i):
-        y = (w // 8 + far(i // 8)) % 4
-        x = (w // 2 + far(i // 2 % 4)) % 4
-        return y * 8 + x * 2 + (w + 1 + i) % 2
+    def flips(value, *weights):
+        return [weight * (1 - 2 * (value // weight % 2)) for weight in weights]
+
+    def flipped(value, steps, k):
+        return value + sum(step for bit, step in enumerate(steps) if k >> bit & 1)
+
+    plane_flips, w_flips = flips(energy, 1, 8, 16, 32, 64), flips(w, 1, 2, 4, 8, 16)
+    depth_flips, zl_flips, zh_flips = flips(energy, 2, 4), flips(zl, 1, 2), flips(zh, 1, 2)
+    plane_peers = [
+        (flipped(w, w_flips, k), {"energy": flipped(energy, plane_flips, k), "elem": zh})
+        for k in PLANE_STEPS
+    ]
+    line_peers = [
+        (
+            flipped(zl, zl_flips, k % 4),
+            flipped(zh, zh_flips, k // 4),
+            {"energy": flipped(energy, depth_flips, k % 4), "elem": flipped(zh, zh_flips, k // 4)},
+        )
+        for k in LINE_STEPS
+    ]
 
     def meet_zl(low):
         return (low + 2) % DEPTH
@@ -156,19 +172,8 @@
 
     barrier = pltpu.get_barrier_semaphore()
 
-    def greet_line(i, c):
-        low, high = line_peer(i)
-        pl.semaphore_signal(barrier, inc=1, device_id=device(w, low, high), device_id_type=MESH)
-        return c
-
-    def greet_plane(i, c):
-        pl.semaphore_signal(
-            barrier, inc=1, device_id=device(plane_peer(i), zl, zh), device_id_type=MESH
-        )
-        return c
-
-    lax.fori_loop(0, LINE - 1, greet_line, 0)
-    lax.fori_loop(0, PLANE - 1, greet_plane, 0)
+    for *_, where in line_peers + plane_peers:
+        pl.semaphore_signal(barrier, inc=1, device_id=where, device_id_type=MESH)
     table_copies = [
         pltpu.make_async_copy(src, dst, table_sem.at[i])
         for i, (src, dst) in enumerate(zip(tables_in, tables_here))
@@ -215,49 +220,34 @@
             send(phase, i, src(low), dst, recv, device(w, low, zh))
         pltpu.make_async_copy(src(zl), dst, recv).start()
 
-    def line_copy(phase, src, dst, recv, i):
-        low, high = line_peer(i)
-        return remote(src(low, high), dst, line_send.at[phase, i], recv, device(w, low, high))
-
     def line(phase, src, dst, recv, make=None):
-        def start(i, c):
-            if make is not None:
-                make(*line_peer(i))
-            line_copy(phase, src, dst, recv, i).start()
-            return c
-
-        lax.fori_loop(0, LINE - 1, start, 0, unroll=3)
-        if make is not None:
+        if make is None:
+            for low, high, where in line_peers:
+                remote(src(low, high), dst, line_send.at[phase], recv, where).start()
+        else:
+
+            def start(i, c):
+                low, high = line_peer(i)
+                make(low, high)
+                remote(
+                    src(low, high), dst, line_send.at[phase], recv, device(w, low, high)
+                ).start()
+                return c
+
+            lax.fori_loop(0, LINE - 1, start, 0, unroll=3)
             make(zl, zh)
         pltpu.make_async_copy(src(zl, zh), dst, recv).start()
 
-    def line_done(phase, src, dst, recv):
-        def done(i, c):
-            line_copy(phase, src, dst, recv, i).wait_send()
-            return c
-
-        lax.fori_loop(0, LINE - 1, done, 0)
-
-    def plane_copy(phase, src, dst, recv, i):
-        other = plane_peer(i)
-        return remote(
-            src(other), dst(w), plane_send.at[phase, i], recv, device(other, zl, zh)
-        )
+    def line_done(phase):
+        arrived(swapped.at[0, :, pl.ds(0, (LINE - 1) * LANES)], line_send.at[phase])
 
     def plane(phase, src, dst, recv):
-        def start(i, c):
-            plane_copy(phase, src, dst, recv, i).start()
-            return c
-
-        lax.fori_loop(0, PLANE - 1, start, 0, unroll=4)
+        for other, where in plane_peers:
+            remote(src(other), dst(w), plane_send.at[phase], recv, where).start()
         pltpu.make_async_copy(src(w), dst(w), recv).start()
 
-    def plane_done(phase, src, dst, recv):
-        def done(i, c):
-            plane_copy(phase, src, dst, recv, i).wait_send()
-            return c
-
-        lax.fori_loop(0, PLANE - 1, done, 0)
+    def plane_done(phase, blocks):
+        arrived(blocks, plane_send.at[phase])
 
     def both_parts(ref):
         return lambda other: ref.at[:, other]
@@ -367,13 +357,13 @@
     lesser_copy.start()
     for copy in started:
         copy.wait_send()
-    plane_done(0, both_parts(send_a), both_parts(mid_a), sems.at[6])
-    plane_done(5, both_parts(send_p), both_parts(got_p), sems.at[11])
-    for part in parts:
-        line_done(part, swapped_src(part), z2_dst(part), sems.at[4 + part])
-        line_done(2 + part, wide_src(part), back_dst(part), sems.at[12 + part])
-        plane_done(1 + part, one_part(send_b, part), one_part(own_b, part), sems.at[7 + part])
-        plane_done(3 + part, one_part(back_q, part), one_part(got_q, part), sems.at[9 + part])
+    plane_done(0, send_a.at[:, pl.ds(0, PLANE - 1)])
+    plane_done(5, send_p.at[:, pl.ds(0, PLANE - 1)])
+    for part in parts:
+        line_done(part)
+        line_done(2 + part)
+        plane_done(1 + part, send_b.at[part, pl.ds(0, PLANE - 1)])
+        plane_done(3 + part, back_q.at[part, pl.ds(0, PLANE - 1)])
     lesser_copy.wait()
     for part in parts:
         arrived(greater_out.at[part], sems.at[15 + part])
@@ -404,8 +394,8 @@
             owned, owned, cut, long, long, freq, deep, sorted_, owned, owned, whole,
             pltpu.SemaphoreType.DMA((6,)),
             pltpu.SemaphoreType.DMA((17,)),
-            pltpu.SemaphoreType.DMA((4, LINE - 1)),
-            pltpu.SemaphoreType.DMA((6, PLANE - 1)),
+            pltpu.SemaphoreType.DMA((4,)),
+            pltpu.SemaphoreType.DMA((6,)),
             pltpu.SemaphoreType.DMA((7, 4)),
         ],
         compiler_params=pltpu.CompilerParams(

time: 70.6 us -> 67.6 us (0.958)
  the two profiles are of different devices: /device:TPU:32 before, /device:TPU:1 now
where the time goes in v4:
time: 67.6 us; the launch traced here: 66.5 us
  Pallas kernels  63.6 us (94%)
  local copies, waits for them, and re-layouts  2.26 us (3%)
    pallas_call x1, Pallas kernels, per_device(): pl.pallas_call(kernel, out_shape=(field, field), in_specs=[anywhere] * 7,...  63.6 us
    unnamed x4, local copies, waits for them, and re-layouts  2.26 us

profile of v4, /device:TPU:1, one launch (start us, length us, event | category | flops | bytes accessed | tf_op | source)
XLA Modules:
  0.0 66.5 jit_solution(6216390566330926063)
XLA Ops:
  0.6 63.6 %shard_map.86 = (f32[2,32,512]{2,1,0:T(8,128)}, f32[2,32,512]{2,1,0:T(8,128)}) custom-call(f32[2,32,512]{2,1,0:T(8,128)} %lesser.1, f32[2,32,512]{2,1,0:T(8,128)} %greater.1, s32[4,1,128]{2,1,0:T(1,128)} %bitcast.1, f32[512,256]{1,0:T(8,128)} %constant.8.clone.refs_0_, f32[256,256]{1,0:T(8,128)} %constant.9.clone.refs_1_, ...), custom_call_target="tpu_custom_call" | custom-call | tf_op jit(solution)/shard_map/pallas_call | solution.py:384
  64.2 0.0 copy-start
  64.2 1.6 %copy.11 = f32[2,32,512]{2,1,0:T(8,128)} copy(f32[2,32,512]{2,1,0:T(8,128)} %get-tuple-element.4) | data formatting | bytes 262144
  65.8 0.0 copy-done
  65.8 0.7 copy.12
Async XLA Ops:
  64.2 1.6 %copy-start = (f32[2,32,512]{2,1,0:T(8,128)S(1)}, f32[2,32,512]{2,1,0:T(8,128)}, u32[]{:S(2)}) copy-start(f32[2,32,512]{2,1,0:T(8,128)} %get-tuple-element.5) | copy-start | bytes 393220

commit v5 on v4

--- a/solution.py
+++ b/solution.py
@@ -126,7 +126,7 @@
     (
         order, z1, swapped, z2, lesser_here, send_a, mid_a, deep_a, own_a, freq_a, send_b, own_b,
         back_q, got_q, wide_q, z2_back, unswapped, freq_p, back_p, mid_p, send_p, got_p, lesser_done,
-        table_sem, sems, line_send, plane_send, few_send,
+        table_sem, sems, line_send, plane_send, few_send, here,
     ) = refs
     energy, zh = lax.axis_index("energy"), lax.axis_index("elem")
     w, zl = energy // 8 * 2 + energy % 2, energy // 2 % DEPTH
@@ -172,7 +172,14 @@
 
     barrier = pltpu.get_barrier_semaphore()
 
-    for *_, where in line_peers + plane_peers:
+    ring = [{"energy": flipped(energy, plane_flips, k), "elem": zh} for k in range(1, 8)]
+    near = [{"energy": flipped(energy, plane_flips, k), "elem": zh} for k in (8, 16, 24)]
+    near += [{"energy": flipped(energy, depth_flips, k), "elem": zh} for k in (1, 3)]
+    near += [
+        {"energy": flipped(energy, depth_flips, 2), "elem": flipped(zh, zh_flips, k)}
+        for k in (2, 1, 3, 0)
+    ]
+    for where in near[::-1] + ring:
         pl.semaphore_signal(barrier, inc=1, device_id=where, device_id_type=MESH)
     table_copies = [
         pltpu.make_async_copy(src, dst, table_sem.at[i])
@@ -185,7 +192,7 @@
     lesser_copy.wait()
     for part in parts:
         to_owner(lambda low: lesser_here[part, :, low * LANES : (low + 1) * LANES], send_a.at[part])
-    pl.semaphore_wait(barrier, LINE - 1 + PLANE - 1)
+    pl.semaphore_wait(barrier, len(near) + len(ring))
 
     def remote(src, dst, send, recv, where):
         return pltpu.make_async_remote_copy(
@@ -267,6 +274,9 @@
         send(0, i, partner, order.at[zh], sems.at[0], device(w, meet_zl(zl), h))
     for part in parts:
         meet(1 + part, lambda h: quarter(greater, part, h), lanes(z1.at[part], zh * 512, 512), sems.at[1 + part])
+    for where in ring:
+        pl.semaphore_signal(here, inc=1, device_id=where, device_id_type=MESH)
+    pl.semaphore_wait(here, len(ring))
     plane(0, both_parts(send_a), both_parts(mid_a), sems.at[6])
     for copy in table_copies:
         copy.wait()
@@ -338,7 +348,7 @@
         arrived(z2_back.at[part], sems.at[12 + part])
         make = make_tile(z2_back.at[part], unswapped.at[part])
         for i in range(GROUPS):
-            h = (zh + 1 + i) % GROUPS
+            h = (zh + 1 + zl // 2 + i) % GROUPS
             for low in range(DEPTH):
                 make(low, h)
             send(
@@ -397,6 +407,7 @@
             pltpu.SemaphoreType.DMA((4,)),
             pltpu.SemaphoreType.DMA((6,)),
             pltpu.SemaphoreType.DMA((7, 4)),
+            pltpu.SemaphoreType.REGULAR,
         ],
         compiler_params=pltpu.CompilerParams(
             collective_id=0, has_side_effects=True, vmem_limit_bytes=56 * 1024 * 1024

time: 67.6 us -> 65.4 us (0.967); the launches traced: 66.5 us -> 65.3 us
  Pallas kernels: 63.6 us -> 62.4 us
    pallas_call x1, Pallas kernels: 63.6 us -> 62.4 us  [per_device(): pl.pallas_call(kernel, out_shape=(field, field), in_specs=[anywhere] * 7,...]
where the time goes in v5:
time: 65.4 us; the launch traced here: 65.3 us
  Pallas kernels  62.4 us (95%)
  local copies, waits for them, and re-layouts  2.26 us (3%)
    pallas_call x1, Pallas kernels, per_device(): pl.pallas_call(kernel, out_shape=(field, field), in_specs=[anywhere] * 7,...  62.4 us
    unnamed x4, local copies, waits for them, and re-layouts  2.26 us

profile of v5, /device:TPU:1, one launch (start us, length us, event | category | flops | bytes accessed | tf_op | source)
XLA Modules:
  0.0 65.3 jit_solution(5639355189335993343)
XLA Ops:
  0.6 62.4 %shard_map.86 = (f32[2,32,512]{2,1,0:T(8,128)}, f32[2,32,512]{2,1,0:T(8,128)}) custom-call(f32[2,32,512]{2,1,0:T(8,128)} %lesser.1, f32[2,32,512]{2,1,0:T(8,128)} %greater.1, s32[4,1,128]{2,1,0:T(1,128)} %bitcast.1, f32[512,256]{1,0:T(8,128)} %constant.8.clone.refs_0_, f32[256,256]{1,0:T(8,128)} %constant.9.clone.refs_1_, ...), custom_call_target="tpu_custom_call" | custom-call | tf_op jit(solution)/shard_map/pallas_call | solution.py:394
  63.0 0.0 copy-start
  63.0 1.6 %copy.11 = f32[2,32,512]{2,1,0:T(8,128)} copy(f32[2,32,512]{2,1,0:T(8,128)} %get-tuple-element.4) | data formatting | bytes 262144
  64.6 0.0 copy-done
  64.6 0.7 %copy.12 = f32[2,32,512]{2,1,0:T(8,128)} copy(f32[2,32,512]{2,1,0:T(8,128)S(1)} %copy-done) | data formatting | bytes 262144
Async XLA Ops:
  63.0 1.6 %copy-start = (f32[2,32,512]{2,1,0:T(8,128)S(1)}, f32[2,32,512]{2,1,0:T(8,128)}, u32[]{:S(2)}) copy-start(f32[2,32,512]{2,1,0:T(8,128)} %get-tuple-element.5) | copy-start | bytes 393220

commit v6 on v5

--- a/solution.py
+++ b/solution.py
@@ -26,8 +26,7 @@
     first = np.concatenate(
         [np.where(part == 0, cos, sin), np.where(part == 0, -sin, cos)], 0
     )
-    scale = 1.0 / (64 * PERIOD)
-    last = scale * np.concatenate(
+    last = np.concatenate(
         [np.where(part == 0, sin, cos).T, np.where(part == 0, -cos, sin).T], 1
     )
     lane = np.arange(LANES)
@@ -344,18 +343,24 @@
         for low in range(DEPTH):
             send_p[part, :, low, :] = mid_p[part, low]
     plane(5, both_parts(send_p), both_parts(got_p), sems.at[11])
+
+    def leave(part, h):
+        make = make_tile(z2_back.at[part], unswapped.at[part])
+        for low in range(DEPTH):
+            make(low, h)
+        send(
+            5 + part, h, lanes(unswapped.at[part], h * 512, 512),
+            quarter(greater_out, part, met_quarter(zl, zh)), sems.at[15 + part],
+            device(w, meet_zl(zl), h),
+        )
+
     for part in parts:
         arrived(z2_back.at[part], sems.at[12 + part])
-        make = make_tile(z2_back.at[part], unswapped.at[part])
-        for i in range(GROUPS):
-            h = (zh + 1 + zl // 2 + i) % GROUPS
-            for low in range(DEPTH):
-                make(low, h)
-            send(
-                5 + part, i, lanes(unswapped.at[part], h * 512, 512),
-                quarter(greater_out, part, met_quarter(zl, zh)), sems.at[15 + part],
-                device(w, meet_zl(zl), h),
-            )
+        for h in (0, 1):
+            leave(part, h)
+    for part in parts:
+        for h in (2, 3):
+            leave(part, h)
     arrived(got_p, sems.at[11])
     for part in parts:
 
@@ -391,7 +396,7 @@
     cut = pltpu.VMEM((2, DEPTH, GROUPS, 8, LANES), f32)
     anywhere = pl.BlockSpec(memory_space=pltpu.HBM)
     constants = [jnp.asarray(table) for table in tables()]
-    return pl.pallas_call(
+    lesser_polar, greater_polar = pl.pallas_call(
         kernel,
         out_shape=(field, field),
         in_specs=[anywhere] * 7,
@@ -413,6 +418,8 @@
             collective_id=0, has_side_effects=True, vmem_limit_bytes=56 * 1024 * 1024
         ),
     )(lesser, greater, partner.reshape(4, 1, LANES), *constants)
+    scale = 1.0 / (64 * PERIOD)
+    return lesser_polar * scale, greater_polar * scale
 
 
 def solution(mesh):

time: 65.4 us -> 64.5 us (0.986)
  local copies, waits for them, and re-layouts: 2.26 us -> 0 us
  other arithmetic: 0 us -> 1.69 us
    unnamed x4 -> x0, local copies, waits for them, and re-layouts: 2.26 us -> none
    mul x0 -> x1, other arithmetic: none -> 1.69 us  [per_device(): return (lesser_polar * scale, greater_polar * scale)]
where the time goes in v6:
time: 64.5 us; the launch traced here: 64.1 us
  Pallas kernels  61.8 us (96%)
  other arithmetic  1.69 us (3%)
    pallas_call x1, Pallas kernels, per_device(): pl.pallas_call(kernel, out_shape=(field, field), in_specs=[anywhere] * 7,...  61.8 us
    mul x1, other arithmetic, per_device(): return (lesser_polar * scale, greater_polar * scale)  1.69 us

profile of v6, /device:TPU:1, one launch (start us, length us, event | category | flops | bytes accessed | tf_op | source)
XLA Modules:
  0.0 64.1 jit_solution(6758713841499607579)
XLA Ops:
  0.6 61.8 %shard_map.86 = (f32[2,32,512]{2,1,0:T(8,128)}, f32[2,32,512]{2,1,0:T(8,128)}) custom-call(f32[2,32,512]{2,1,0:T(8,128)} %lesser.1, f32[2,32,512]{2,1,0:T(8,128)} %greater.1, s32[4,1,128]{2,1,0:T(1,128)} %bitcast.1, f32[512,256]{1,0:T(8,128)} %constant.10.clone.refs_0_, f32[256,256]{1,0:T(8,128)} %constant.11.clone.refs_1_, ...), custom_call_target="tpu_custom_call" | custom-call | tf_op jit(solution)/shard_map/pallas_call | solution.py:399
  62.4 1.7 %broadcast_multiply_fusion = (f32[2,32,512]{2,1,0:T(8,128)}, f32[2,32,512]{2,1,0:T(8,128)}) fusion(f32[2,32,512]{2,1,0:T(8,128)} %get-tuple-element.5, f32[2,32,512]{2,1,0:T(8,128)} %get-tuple-element.4), kind=kLoop, calls=%fused_computation | loop fusion | flops 65536 | bytes 524288 | tf_op jit(solution)/shard_map/mul | solution.py:422

commit v7 on v6

--- a/solution.py
+++ b/solution.py
@@ -317,50 +317,41 @@
     for part in parts:
         for low in range(DEPTH):
             back_q[part, :, low, :] = q[part * LANES + low * PLANE : part * LANES + (low + 1) * PLANE]
-        plane(3 + part, one_part(back_q, part), one_part(got_q, part), sems.at[9 + part])
+    plane(3, both_parts(back_q), both_parts(got_q), sems.at[9])
     p = inverse(freq_p[...], middle(), last(), turn[0], turn[1])
     for low in range(DEPTH):
         back_p[low, 0] = -p[low * PLANE : (low + 1) * PLANE]
         back_p[low, 1] = p[LANES + low * PLANE : LANES + (low + 1) * PLANE]
     depths(4, lambda low: back_p.at[low], mid_p.at[:, zl], sems.at[14])
 
-    def wide_src(part):
-        return lambda low, high: wide_q.at[part, meet_zl(low), met_quarter(low, high)]
-
-    def back_dst(part):
-        return lanes(z2_back.at[part], z * LANES, LANES)
-
-    for part in parts:
-        arrived(got_q.at[part], sems.at[9 + part])
+    arrived(got_q, sems.at[9])
+    for part in parts:
 
         def keep_q(low, rows):
             wide_q[part, low] = rows.reshape(GROUPS, 8, LANES)
 
         to_energies(got_q.at[part], keep_q)
-        line(2 + part, wide_src(part), back_dst(part), sems.at[12 + part])
+    line(
+        2, lambda low, high: wide_q.at[:, meet_zl(low), met_quarter(low, high)],
+        lanes(z2_back, z * LANES, LANES), sems.at[12],
+    )
     arrived(mid_p, sems.at[14])
     for part in parts:
         for low in range(DEPTH):
             send_p[part, :, low, :] = mid_p[part, low]
     plane(5, both_parts(send_p), both_parts(got_p), sems.at[11])
 
-    def leave(part, h):
-        make = make_tile(z2_back.at[part], unswapped.at[part])
-        for low in range(DEPTH):
-            make(low, h)
+    arrived(z2_back, sems.at[12])
+    for h in range(GROUPS):
+        for part in parts:
+            make = make_tile(z2_back.at[part], unswapped.at[part])
+            for low in range(DEPTH):
+                make(low, h)
+        rows = pl.ds(pl.multiple_of(met_quarter(zl, zh) * 8, 8), 8)
         send(
-            5 + part, h, lanes(unswapped.at[part], h * 512, 512),
-            quarter(greater_out, part, met_quarter(zl, zh)), sems.at[15 + part],
+            5, h, lanes(unswapped, h * 512, 512), greater_out.at[:, rows, :], sems.at[15],
             device(w, meet_zl(zl), h),
         )
-
-    for part in parts:
-        arrived(z2_back.at[part], sems.at[12 + part])
-        for h in (0, 1):
-            leave(part, h)
-    for part in parts:
-        for h in (2, 3):
-            leave(part, h)
     arrived(got_p, sems.at[11])
     for part in parts:
 
@@ -373,15 +364,14 @@
     for copy in started:
         copy.wait_send()
     plane_done(0, send_a.at[:, pl.ds(0, PLANE - 1)])
+    plane_done(3, back_q.at[:, pl.ds(0, PLANE - 1)])
+    arrived(swapped.at[:, :, pl.ds(0, (LINE - 1) * LANES)], line_send.at[2])
     plane_done(5, send_p.at[:, pl.ds(0, PLANE - 1)])
     for part in parts:
         line_done(part)
-        line_done(2 + part)
         plane_done(1 + part, send_b.at[part, pl.ds(0, PLANE - 1)])
-        plane_done(3 + part, back_q.at[part, pl.ds(0, PLANE - 1)])
     lesser_copy.wait()
-    for part in parts:
-        arrived(greater_out.at[part], sems.at[15 + part])
+    arrived(greater_out, sems.at[15])
 
 
 def per_device(lesser, greater, partner):

time: 64.5 us -> 64.6 us (level)
  no operation moved by 1% of the time
where the time goes in v7:
time: 64.6 us; the launch traced here: 64.3 us
  Pallas kernels  61.9 us (96%)
  other arithmetic  1.69 us (3%)
    pallas_call x1, Pallas kernels, per_device(): pl.pallas_call(kernel, out_shape=(field, field), in_specs=[anywhere] * 7,...  61.9 us
    mul x1, other arithmetic, per_device(): return (lesser_polar * scale, greater_polar * scale)  1.69 us

profile of v7, /device:TPU:1, one launch (start us, length us, event | category | flops | bytes accessed | tf_op | source)
XLA Modules:
  0.0 64.3 jit_solution(7094789899462740342)
XLA Ops:
  0.6 61.9 %shard_map.86 = (f32[2,32,512]{2,1,0:T(8,128)}, f32[2,32,512]{2,1,0:T(8,128)}) custom-call(f32[2,32,512]{2,1,0:T(8,128)} %lesser.1, f32[2,32,512]{2,1,0:T(8,128)} %greater.1, s32[4,1,128]{2,1,0:T(1,128)} %bitcast.1, f32[512,256]{1,0:T(8,128)} %constant.10.clone.refs_0_, f32[256,256]{1,0:T(8,128)} %constant.11.clone.refs_1_, ...), custom_call_target="tpu_custom_call" | custom-call | tf_op jit(solution)/shard_map/pallas_call | solution.py:389
  62.6 1.7 %broadcast_multiply_fusion = (f32[2,32,512]{2,1,0:T(8,128)}, f32[2,32,512]{2,1,0:T(8,128)}) fusion(f32[2,32,512]{2,1,0:T(8,128)} %get-tuple-element.5, f32[2,32,512]{2,1,0:T(8,128)} %get-tuple-element.4), kind=kLoop, calls=%fused_computation | loop fusion | flops 65536 | bytes 524288 | tf_op jit(solution)/shard_map/mul | solution.py:412
